TPU v7x, 32 devices: a whole 2x2x4 slice. The times are simulated.
32 devices in a mesh: freq: 8 (over z, y), sta: 4 (over x, core).
Axes of the slice: x: 2, y: 2, z: 4, core: 2. Of those that a mesh axis runs over, the one named last changes fastest.
Arguments:
- spectra: float32 [2, 128, 64, 8192], P(None, 'freq', None, 'sta'), may hold values from -24 to 24
- current: float32 [64, 2, 128, 512], P('freq', None, None, 'sta'), may hold values from -600 to 600, as said below
- previous: float32 [64, 2, 128, 512], P('freq', None, None, 'sta'), may hold values from -600 to 600, as said below
- table: int32 [64, 512], replicated, may hold values from 0 to 16383
- station_block: int32 [8192], P('sta'), may hold values from 0 to 63
- offsets: float32 [2, 8192], P(None, 'sta'), may hold values from -4 to 4
- slowness: float32 [2, 512], replicated, may hold values from -3 to 3
- weights: float32 [512], P('sta'), may hold values from 400 to 5000
- momentum: float32 [1], replicated, may hold values from 2 to 10
Outputs:
- estimate: float32 [64, 2, 128, 512], P('freq', None, None, 'sta')
- extrapolated: float32 [64, 2, 128, 512], P('freq', None, None, 'sta')
Inputs may be any that keep to these rules, and one draw needn't show every extreme that they name: `current`: real values. `previous`: real values.
All inputs are finite; a program needn't handle non-finite values.
Results may differ from a plain program's by a relative error of at most 0.00105.
The roundings to bfloat16 on the way count: a program that leaves them out, or rounds other values in their place, can miss the bound.
Values may be sent and summed in bfloat16 or wider, within the bound.
A program may use at most 192 MiB of HBM per device.

v0:
```python
import math
import jax
import jax.numpy as jnp
from jax import lax
from jax.sharding import PartitionSpec as P

F = 64
CELLS = 512


def cell_block(cell_count):
    block_len = cell_count
    while block_len > 512 and block_len % 2 == 0:
        block_len = block_len // 2
    return block_len


def phases(number, delay_rows, off_rows, slow_cols, period):
    wrapped = number * delay_rows % period
    geometry = (
        off_rows[0][:, None] * slow_cols[0][None, :] + off_rows[1][:, None] * slow_cols[1][None, :]
    )
    phase_angle = (wrapped.astype(jnp.float32) + number.astype(jnp.float32) * geometry) * (
        2.0 * math.pi / period
    )
    return (jnp.cos(phase_angle).astype(jnp.bfloat16), jnp.sin(phase_angle).astype(jnp.bfloat16))


def forward_terms(cos_part, sin_part, iterate):
    window_count = iterate.shape[1]
    stacked = iterate.reshape(2 * window_count, iterate.shape[2])
    contract = (((1,), (1,)), ((), ()))
    with_cos = lax.dot_general(stacked, cos_part, contract, preferred_element_type=jnp.float32)
    with_sin = lax.dot_general(stacked, sin_part, contract, preferred_element_type=jnp.float32)
    real_part = with_cos[:window_count] + with_sin[window_count:]
    imag_part = with_cos[window_count:] - with_sin[:window_count]
    return jnp.stack([real_part, imag_part])


def adjoint_terms(cos_part, sin_part, residual):
    window_count = residual.shape[1]
    stacked = residual.reshape(2 * window_count, residual.shape[2])
    with_cos = jnp.dot(stacked, cos_part, preferred_element_type=jnp.float32)
    with_sin = jnp.dot(stacked, sin_part, preferred_element_type=jnp.float32)
    real_part = with_cos[:window_count] - with_sin[window_count:]
    imag_part = with_cos[window_count:] + with_sin[:window_count]
    return jnp.stack([real_part, imag_part])


def local(spectra, current, previous, table, station_block, offsets, slowness, weights, momentum):
    period = 4 * F
    normalizer = 1.0 / math.sqrt(CELLS)
    bin_count = current.shape[0]
    cell_share = current.shape[3]
    stations_here = station_block.shape[0]
    station_total = stations_here * lax.axis_size("sta")
    first_bin = lax.axis_index("freq") * bin_count
    relaid = lax.all_to_all(
        spectra.astype(jnp.bfloat16), "freq", split_axis=2, concat_axis=1, tiled=True
    ).astype(spectra.dtype)
    iterate_b = current.astype(jnp.bfloat16)
    segment = lax.all_gather(iterate_b, "sta", axis=3, tiled=True)
    cell_count = segment.shape[3]
    block_len = cell_block(cell_count)
    delay_rows = jnp.take(table, station_block, axis=0)
    bin_terms = []
    cos_blocks = []
    sin_blocks = []
    for add_bin_index in range(bin_count):
        cos_part, sin_part = phases(
            first_bin + add_bin_index + 1, delay_rows, offsets, slowness, period
        )
        cos_blocks.append(cos_part)
        sin_blocks.append(sin_part)
        bin_terms.append(
            forward_terms(cos_part, sin_part, segment[add_bin_index, :, :, 0:block_len])
        )
    running = jnp.stack(bin_terms)
    cos_all = jnp.stack(cos_blocks)
    sin_all = jnp.stack(sin_blocks)
    predicted, cos_all, sin_all = (running, cos_all, sin_all)
    bin_sums = []
    for bin_index in range(bin_count):
        residual = (predicted[bin_index] * normalizer - relaid[:, :, bin_index, :]).astype(
            jnp.bfloat16
        )
        bin_sums.append(
            adjoint_terms(cos_all[bin_index], sin_all[bin_index], residual) * normalizer
        )
    partial_sums = jnp.stack(bin_sums)
    summed = lax.psum(partial_sums, "sta")
    gradient = lax.dynamic_slice_in_dim(summed, lax.axis_index("sta") * cell_share, cell_share, 3)
    step_size = CELLS / (math.sqrt(station_total) + math.sqrt(CELLS)) ** 2
    stepped = current - step_size * gradient
    threshold = step_size * weights
    squares = jnp.sum(stepped * stepped, axis=(0, 1))
    group_norm = jnp.sqrt(lax.psum(squares, "freq") + 1e-06)
    estimate = stepped * jnp.maximum(0.0, 1.0 - threshold[None, :] / group_norm)
    momentum_now = momentum[0]
    momentum_next = (1.0 + jnp.sqrt(1.0 + 4.0 * momentum_now * momentum_now)) / 2.0
    extrapolated = estimate + (momentum_now - 1.0) / momentum_next * (estimate - previous)
    return (estimate, extrapolated)


def solution(mesh):
    in_specs = (
        P(None, "freq", None, "sta"),
        P("freq", None, None, "sta"),
        P("freq", None, None, "sta"),
        P(),
        P("sta"),
        P(None, "sta"),
        P(),
        P("sta"),
        P(),
    )
    out_specs = (P("freq", None, None, "sta"), P("freq", None, None, "sta"))
    return jax.shard_map(local, mesh=mesh, in_specs=in_specs, out_specs=out_specs, check_vma=False)
```

profile of v0, /device:TPU:0, one launch (start us, length us, event | category | flops | bytes accessed | tf_op | source)
XLA Modules:
  0.0 836.7 jit_solution(6741037382420943036)
XLA Ops:
  9.4 17.2 %copy.25 = bf16[2,16,64,2048]{3,1,0,2:T(8,128)(2,1)} copy(f32[2,16,64,2048]{3,2,1,0:T(8,128)} %param.9) | data formatting | bytes 25165824 | tf_op args[0]
  43.6 18.0 %fusion.31 = (f32[2048,512]{1,0:T(8,128)}, f32[2048,512]{1,0:T(8,128)}, f32[2048,512]{1,0:T(8,128)}, f32[2048,512]{1,0:T(8,128)}, f32[2048,512]{1,0:T(8,128)}, /*index=5*/f32[2048,512]{1,0:T(8,128)}) fusion(s32[2048,512]{1,0:T(8,128)} %gather_fusion, f32[]{:T(128)S(6)} %convert_element_type.188, s32[]{:T(128)S(6)} %add.230, f32[512]{0:T(512)S(1)} %bitcast.221, ...), kind=kLoop, calls=%fused_computation.58 | loop fusion | flops 104857600 | bytes 29382704 | tf_op jit(solution)/shard_map/mul | solution.py:23
  73.1 15.0 %convolution_bitcast_fusion.2 = f32[256,2048]{1,0:T(8,128)S(1)} fusion(bf16[256,512]{1,0:T(8,128)(2,1)S(1)} %bitcast.213, f32[2048,512]{1,0:T(8,128)S(1)} %copy-done.16), kind=kOutput, calls=%fused_computation.78 | convolution fusion | flops 537919488 | bytes 6553600 | tf_op jit(solution)/shard_map/dot_general | solution.py:34
  88.2 14.9 %convolution_bitcast_fusion.3 = f32[256,2048]{1,0:T(8,128)S(1)} fusion(bf16[256,512]{1,0:T(8,128)(2,1)S(1)} %bitcast.214, f32[2048,512]{1,0:T(8,128)S(1)} %copy-done.16), kind=kOutput, calls=%fused_computation.79 | convolution fusion | flops 537919488 | bytes 6553600 | tf_op jit(solution)/shard_map/dot_general | solution.py:33
  106.0 15.0 %convolution_bitcast_fusion.14 = f32[256,2048]{1,0:T(8,128)S(1)} fusion(bf16[256,512]{1,0:T(8,128)(2,1)S(1)} %bitcast.211, f32[2048,512]{1,0:T(8,128)S(1)} %copy-done.14), kind=kOutput, calls=%fused_computation.90 | convolution fusion | flops 537919488 | bytes 6553600 | tf_op jit(solution)/shard_map/dot_general | solution.py:34
  121.0 15.1 %convolution_bitcast_fusion.15 = f32[256,2048]{1,0:T(8,128)S(1)} fusion(bf16[256,512]{1,0:T(8,128)(2,1)S(1)} %bitcast.212, f32[2048,512]{1,0:T(8,128)S(1)} %copy-done.14), kind=kOutput, calls=%fused_computation.91 | convolution fusion | flops 537919488 | bytes 6553600 | tf_op jit(solution)/shard_map/dot_general | solution.py:33
  137.9 15.0 %convolution_bitcast_fusion = f32[256,2048]{1,0:T(8,128)S(1)} fusion(bf16[256,512]{1,0:T(8,128)(2,1)S(1)} %bitcast.209, f32[2048,512]{1,0:T(8,128)S(1)} %copy-done.12), kind=kOutput, calls=%fused_computation.76 | convolution fusion | flops 537919488 | bytes 6553600 | tf_op jit(solution)/shard_map/dot_general | solution.py:34
  152.9 14.9 %convolution_bitcast_fusion.1 = f32[256,2048]{1,0:T(8,128)S(1)} fusion(bf16[256,512]{1,0:T(8,128)(2,1)S(1)} %bitcast.210, f32[2048,512]{1,0:T(8,128)S(1)} %copy-done.12), kind=kOutput, calls=%fused_computation.77 | convolution fusion | flops 537919488 | bytes 6553600 | tf_op jit(solution)/shard_map/dot_general | solution.py:33
  169.9 15.0 %convolution_bitcast_fusion.12 = f32[256,2048]{1,0:T(8,128)S(1)} fusion(bf16[256,512]{1,0:T(8,128)(2,1)S(1)} %bitcast.207, f32[2048,512]{1,0:T(8,128)S(1)} %copy-done.10), kind=kOutput, calls=%fused_computation.88 | convolution fusion | flops 537919488 | bytes 6553600 | tf_op jit(solution)/shard_map/dot_general | solution.py:34
  184.9 14.9 %convolution_bitcast_fusion.13 = f32[256,2048]{1,0:T(8,128)S(1)} fusion(bf16[256,512]{1,0:T(8,128)(2,1)S(1)} %bitcast.208, f32[2048,512]{1,0:T(8,128)S(1)} %copy-done.10), kind=kOutput, calls=%fused_computation.89 | convolution fusion | flops 537919488 | bytes 6553600 | tf_op jit(solution)/shard_map/dot_general | solution.py:33
  201.6 15.2 %convolution_bitcast_fusion.10 = f32[256,2048]{1,0:T(8,128)S(1)} fusion(bf16[256,512]{1,0:T(8,128)(2,1)S(1)} %bitcast.205, f32[2048,512]{1,0:T(8,128)S(1)} %copy-done.8), kind=kOutput, calls=%fused_computation.86 | convolution fusion | flops 537919488 | bytes 6553600 | tf_op jit(solution)/shard_map/dot_general | solution.py:34
  216.8 14.9 %convolution_bitcast_fusion.11 = f32[256,2048]{1,0:T(8,128)S(1)} fusion(bf16[256,512]{1,0:T(8,128)(2,1)S(1)} %bitcast.206, f32[2048,512]{1,0:T(8,128)S(1)} %copy-done.8), kind=kOutput, calls=%fused_computation.87 | convolution fusion | flops 537919488 | bytes 6553600 | tf_op jit(solution)/shard_map/dot_general | solution.py:33
  233.6 15.0 %convolution_bitcast_fusion.8 = f32[256,2048]{1,0:T(8,128)S(1)} fusion(bf16[256,512]{1,0:T(8,128)(2,1)S(1)} %bitcast.203, f32[2048,512]{1,0:T(8,128)S(1)} %copy-done.6), kind=kOutput, calls=%fused_computation.84 | convolution fusion | flops 537919488 | bytes 6553600 | tf_op jit(solution)/shard_map/dot_general | solution.py:34
  248.6 14.9 %convolution_bitcast_fusion.9 = f32[256,2048]{1,0:T(8,128)S(1)} fusion(bf16[256,512]{1,0:T(8,128)(2,1)S(1)} %bitcast.204, f32[2048,512]{1,0:T(8,128)S(1)} %copy-done.6), kind=kOutput, calls=%fused_computation.85 | convolution fusion | flops 537919488 | bytes 6553600 | tf_op jit(solution)/shard_map/dot_general | solution.py:33
  265.4 15.0 %convolution_bitcast_fusion.6 = f32[256,2048]{1,0:T(8,128)S(1)} fusion(bf16[256,512]{1,0:T(8,128)(2,1)S(1)} %bitcast.201, f32[2048,512]{1,0:T(8,128)S(1)} %copy-done.4), kind=kOutput, calls=%fused_computation.82 | convolution fusion | flops 537919488 | bytes 6553600 | tf_op jit(solution)/shard_map/dot_general | solution.py:34
  280.4 15.3 %convolution_bitcast_fusion.7 = f32[256,2048]{1,0:T(8,128)S(1)} fusion(bf16[256,512]{1,0:T(8,128)(2,1)S(1)} %bitcast.202, f32[2048,512]{1,0:T(8,128)S(1)} %copy-done.4), kind=kOutput, calls=%fused_computation.83 | convolution fusion | flops 537919488 | bytes 6553600 | tf_op jit(solution)/shard_map/dot_general | solution.py:33
  297.7 15.0 %convolution_bitcast_fusion.4 = f32[256,2048]{1,0:T(8,128)S(1)} fusion(bf16[256,512]{1,0:T(8,128)(2,1)S(1)} %bitcast.199, f32[2048,512]{1,0:T(8,128)S(1)} %copy-done.2), kind=kOutput, calls=%fused_computation.80 | convolution fusion | flops 537919488 | bytes 6553600 | tf_op jit(solution)/shard_map/dot_general | solution.py:34
  312.7 14.9 %convolution_bitcast_fusion.5 = f32[256,2048]{1,0:T(8,128)S(1)} fusion(bf16[256,512]{1,0:T(8,128)(2,1)S(1)} %bitcast.200, f32[2048,512]{1,0:T(8,128)S(1)} %copy-done.2), kind=kOutput, calls=%fused_computation.81 | convolution fusion | flops 537919488 | bytes 6553600 | tf_op jit(solution)/shard_map/dot_general | solution.py:33
  329.5 14.0 %convert_bitcast_fusion = f32[2,8,16,8,2048]{4,3,1,2,0:T(8,128)} fusion(bf16[2,16,64,2048]{3,1,0,2:T(8,128)(2,1)} %all-to-all-done), kind=kLoop, calls=%fused_computation.1 | loop fusion | flops 4194304 | bytes 25165824 | tf_op jit(solution)/shard_map/convert_element_type | solution.py:60
  355.4 59.7 %fusion.97 = (f32[2,128,1,2048]{3,2,1,0:T(1,128)}, f32[2,128,1,2048]{3,2,1,0:T(1,128)}, f32[2,128,1,2048]{3,2,1,0:T(1,128)S(1)}, f32[2,128,1,2048]{3,2,1,0:T(1,1...) fusion(f32[2,128,8,2048]{3,2,1,0:T(8,128)} %bitcast.198), kind=kLoop, calls=%fused_computation.221 | loop fusion | bytes 33554432 | tf_op jit(solution)/shard_map/slice | solution.py:84
  448.5 14.0 %fusion.57 = f32[256,512]{1,0:T(8,128)S(1)} fusion(bf16[256,2048]{1,0:T(8,128)(2,1)S(1)} %fusion.39, f32[2048,512]{1,0:T(8,128)S(1)} %copy-done.15), kind=kOutput, calls=%fused_computation.152 | convolution fusion | flops 537919488 | bytes 5767168 | tf_op jit(solution)/shard_map/dot_general | solution.py:44
  462.6 14.2 %fusion.56 = f32[256,512]{1,0:T(8,128)S(1)} fusion(bf16[256,2048]{1,0:T(8,128)(2,1)S(1)} %fusion.39, f32[2048,512]{1,0:T(8,128)S(1)} %copy-done.15), kind=kOutput, calls=%fused_computation.151 | convolution fusion | flops 537919488 | bytes 5767168 | tf_op jit(solution)/shard_map/dot_general | solution.py:43
  479.0 14.0 %fusion.71 = f32[256,512]{1,0:T(8,128)S(1)} fusion(bf16[256,2048]{1,0:T(8,128)(2,1)S(1)} %fusion.32, f32[2048,512]{1,0:T(8,128)S(1)} %copy-done.13), kind=kOutput, calls=%fused_computation.166 | convolution fusion | flops 537919488 | bytes 5767168 | tf_op jit(solution)/shard_map/dot_general | solution.py:44
  509.1 14.0 %fusion.59 = f32[256,512]{1,0:T(8,128)S(1)} fusion(bf16[256,2048]{1,0:T(8,128)(2,1)S(1)} %fusion.38, f32[2048,512]{1,0:T(8,128)S(1)} %copy-done.11), kind=kOutput, calls=%fused_computation.154 | convolution fusion | flops 537919488 | bytes 5767168 | tf_op jit(solution)/shard_map/dot_general | solution.py:44
  523.2 14.2 %fusion.58 = f32[256,512]{1,0:T(8,128)S(1)} fusion(bf16[256,2048]{1,0:T(8,128)(2,1)S(1)} %fusion.38, f32[2048,512]{1,0:T(8,128)S(1)} %copy-done.11), kind=kOutput, calls=%fused_computation.153 | convolution fusion | flops 537919488 | bytes 5767168 | tf_op jit(solution)/shard_map/dot_general | solution.py:43
  539.5 14.0 %fusion.61 = f32[256,512]{1,0:T(8,128)S(1)} fusion(bf16[256,2048]{1,0:T(8,128)(2,1)S(1)} %fusion.37, f32[2048,512]{1,0:T(8,128)S(1)} %copy-done.9), kind=kOutput, calls=%fused_computation.156 | convolution fusion | flops 537919488 | bytes 5767168 | tf_op jit(solution)/shard_map/dot_general | solution.py:44
  569.7 14.0 %fusion.63 = f32[256,512]{1,0:T(8,128)S(1)} fusion(bf16[256,2048]{1,0:T(8,128)(2,1)S(1)} %fusion.36, f32[2048,512]{1,0:T(8,128)S(1)} %copy-done.7), kind=kOutput, calls=%fused_computation.158 | convolution fusion | flops 537919488 | bytes 5767168 | tf_op jit(solution)/shard_map/dot_general | solution.py:44
  583.7 14.2 %fusion.62 = f32[256,512]{1,0:T(8,128)S(1)} fusion(bf16[256,2048]{1,0:T(8,128)(2,1)S(1)} %fusion.36, f32[2048,512]{1,0:T(8,128)S(1)} %copy-done.7), kind=kOutput, calls=%fused_computation.157 | convolution fusion | flops 537919488 | bytes 5767168 | tf_op jit(solution)/shard_map/dot_general | solution.py:43
  630.2 14.0 %fusion.67 = f32[256,512]{1,0:T(8,128)S(1)} fusion(bf16[256,2048]{1,0:T(8,128)(2,1)S(1)} %fusion.34, f32[2048,512]{1,0:T(8,128)S(1)} %copy-done.3), kind=kOutput, calls=%fused_computation.162 | convolution fusion | flops 537919488 | bytes 5767168 | tf_op jit(solution)/shard_map/dot_general | solution.py:44
  644.3 14.0 %fusion.66 = f32[256,512]{1,0:T(8,128)S(1)} fusion(bf16[256,2048]{1,0:T(8,128)(2,1)S(1)} %fusion.34, f32[2048,512]{1,0:T(8,128)S(1)} %copy-done.3), kind=kOutput, calls=%fused_computation.161 | convolution fusion | flops 537919488 | bytes 5767168 | tf_op jit(solution)/shard_map/dot_general | solution.py:43
  666.0 86.9 %all-reduce.3.cloned.1.call-done = f32[8,2,128,512]{3,2,1,0:T(8,128)} async-done(((f32[8,2,128,512]{3,2,1,0:T(8,128)}), f32[8,2,128,512]{3,2,1,0:T(8,128)}) %all-reduce.3.cloned.1.call-update) | async-done | bytes 4194320 | tf_op jit(solution)/shard_map/psum | solution.py:91
  755.7 70.3 %all-reduce.5.cloned.1.call-done = f32[128,128]{1,0:T(8,128)} async-done(((f32[128,128]{1,0:T(8,128)}), f32[128,128]{1,0:T(8,128)}) %all-reduce.5.cloned.1.call-update) | async-done | bytes 65552 | tf_op jit(solution)/shard_map/psum | solution.py:97
  (152 shorter events, 174.1 us)
Async XLA Ops:
  7.2 27.5 %copy-start = (s32[64,512]{1,0:T(8,128)S(1)}, s32[64,512]{1,0:T(8,128)}, u32[]{:S(2)}) copy-start(s32[64,512]{1,0:T(8,128)} %param.12) | copy-start | bytes 393220
  7.2 63.1 %all-gather.2.cloned.1.call-start = ((), (), s32[]{:S(2)}) async-start(), calls=%async_computation.1 | async-start | bytes 2621440 | tf_op jit(solution)/shard_map/all_gather | solution.py:62
  26.6 8.0 copy-start.34
  26.6 8.1 copy-start.36
  26.6 8.1 copy-start.35
  26.6 302.9 %all-to-all-start = ((bf16[2,16,64,2048]{3,1,0,2:T(8,128)(2,1)}), bf16[2,16,64,2048]{3,1,0,2:T(8,128)(2,1)}, u32[]{:S(2)}, u32[]{:S(2)}) async-start(bf16[2,16,64,2048]{3,1,0,2:T(8,128)(2,1)} %copy.25), calls=%async_computation | async-start | bytes 16777216 | tf_op jit(solution)/shard_map/all_to_all | solution.py:58
  34.0 719.0 %all-reduce.3.cloned.1.call-start = ((), (), s32[]{:S(2)}) async-start(), calls=%async_computation.2 | async-start | bytes 8388608 | tf_op jit(solution)/shard_map/psum | solution.py:91
  121.0 16.9 %copy-start.12 = (f32[2048,512]{1,0:T(8,128)S(1)}, f32[2048,512]{1,0:T(8,128)}, u32[]{:S(2)}) copy-start(f32[2048,512]{1,0:T(8,128)} %get-tuple-element.12) | copy-start | bytes 12582916
  152.9 16.9 %copy-start.10 = (f32[2048,512]{1,0:T(8,128)S(1)}, f32[2048,512]{1,0:T(8,128)}, u32[]{:S(2)}) copy-start(f32[2048,512]{1,0:T(8,128)} %get-tuple-element.13) | copy-start | bytes 12582916
  184.9 16.7 %copy-start.8 = (f32[2048,512]{1,0:T(8,128)S(1)}, f32[2048,512]{1,0:T(8,128)}, u32[]{:S(2)}) copy-start(f32[2048,512]{1,0:T(8,128)} %get-tuple-element.14) | copy-start | bytes 12582916
  216.8 16.8 %copy-start.6 = (f32[2048,512]{1,0:T(8,128)S(1)}, f32[2048,512]{1,0:T(8,128)}, u32[]{:S(2)}) copy-start(f32[2048,512]{1,0:T(8,128)} %get-tuple-element.15) | copy-start | bytes 12582916
  248.6 16.8 %copy-start.4 = (f32[2048,512]{1,0:T(8,128)S(1)}, f32[2048,512]{1,0:T(8,128)}, u32[]{:S(2)}) copy-start(f32[2048,512]{1,0:T(8,128)} %get-tuple-element.16) | copy-start | bytes 12582916
  280.4 17.2 %copy-start.2 = (f32[2048,512]{1,0:T(8,128)S(1)}, f32[2048,512]{1,0:T(8,128)}, u32[]{:S(2)}) copy-start(f32[2048,512]{1,0:T(8,128)} %get-tuple-element.17) | copy-start | bytes 12582916
  415.1 3.4 copy-start.17
  432.4 13.9 %copy-start.24 = (f32[2,128,1,2048]{3,2,1,0:T(1,128)S(1)}, f32[2,128,1,2048]{3,2,1,0:T(1,128)}, u32[]{:S(2)}) copy-start(f32[2,128,1,2048]{3,2,1,0:T(1,128)} %get-tuple-element.11) | copy-start | bytes 6291460
  432.4 14.9 %copy-start.26 = (f32[2,128,2048]{2,1,0:T(8,128)S(1)}, f32[2,128,2048]{2,1,0:T(8,128)}, u32[]{:S(2)}) copy-start(f32[2,128,2048]{2,1,0:T(8,128)} %maximum_multiply_fusion) | copy-start | bytes 6291460
  462.6 14.2 %copy-start.23 = (f32[2,128,1,2048]{3,2,1,0:T(1,128)S(1)}, f32[2,128,1,2048]{3,2,1,0:T(1,128)}, u32[]{:S(2)}) copy-start(f32[2,128,1,2048]{3,2,1,0:T(1,128)} %get-tuple-element.4) | copy-start | bytes 6291460
  462.6 15.1 %copy-start.27 = (f32[2,128,2048]{2,1,0:T(8,128)S(1)}, f32[2,128,2048]{2,1,0:T(8,128)}, u32[]{:S(2)}) copy-start(f32[2,128,2048]{2,1,0:T(8,128)} %maximum_multiply_fusion.7) | copy-start | bytes 6291460
  492.9 13.9 %copy-start.22 = (f32[2,128,1,2048]{3,2,1,0:T(1,128)S(1)}, f32[2,128,1,2048]{3,2,1,0:T(1,128)}, u32[]{:S(2)}) copy-start(f32[2,128,1,2048]{3,2,1,0:T(1,128)} %get-tuple-element.10) | copy-start | bytes 6291460
  493.0 14.9 %copy-start.28 = (f32[2,128,2048]{2,1,0:T(8,128)S(1)}, f32[2,128,2048]{2,1,0:T(8,128)}, u32[]{:S(2)}) copy-start(f32[2,128,2048]{2,1,0:T(8,128)} %maximum_multiply_fusion.1) | copy-start | bytes 6291460
  523.1 14.2 %copy-start.21 = (f32[2,128,1,2048]{3,2,1,0:T(1,128)S(1)}, f32[2,128,1,2048]{3,2,1,0:T(1,128)}, u32[]{:S(2)}) copy-start(f32[2,128,1,2048]{3,2,1,0:T(1,128)} %get-tuple-element.9) | copy-start | bytes 6291460
  523.2 15.1 %copy-start.29 = (f32[2,128,2048]{2,1,0:T(8,128)S(1)}, f32[2,128,2048]{2,1,0:T(8,128)}, u32[]{:S(2)}) copy-start(f32[2,128,2048]{2,1,0:T(8,128)} %maximum_multiply_fusion.2) | copy-start | bytes 6291460
  553.5 13.9 %copy-start.20 = (f32[2,128,1,2048]{3,2,1,0:T(1,128)S(1)}, f32[2,128,1,2048]{3,2,1,0:T(1,128)}, u32[]{:S(2)}) copy-start(f32[2,128,1,2048]{3,2,1,0:T(1,128)} %get-tuple-element.8) | copy-start | bytes 6291460
  553.5 14.9 %copy-start.30 = (f32[2,128,2048]{2,1,0:T(8,128)S(1)}, f32[2,128,2048]{2,1,0:T(8,128)}, u32[]{:S(2)}) copy-start(f32[2,128,2048]{2,1,0:T(8,128)} %maximum_multiply_fusion.3) | copy-start | bytes 6291460
  583.7 14.2 %copy-start.19 = (f32[2,128,1,2048]{3,2,1,0:T(1,128)S(1)}, f32[2,128,1,2048]{3,2,1,0:T(1,128)}, u32[]{:S(2)}) copy-start(f32[2,128,1,2048]{3,2,1,0:T(1,128)} %get-tuple-element.7) | copy-start | bytes 6291460
  583.7 15.1 %copy-start.31 = (f32[2,128,2048]{2,1,0:T(8,128)S(1)}, f32[2,128,2048]{2,1,0:T(8,128)}, u32[]{:S(2)}) copy-start(f32[2,128,2048]{2,1,0:T(8,128)} %maximum_multiply_fusion.4) | copy-start | bytes 6291460
  614.1 14.8 %copy-start.32 = (f32[2,128,2048]{2,1,0:T(8,128)S(1)}, f32[2,128,2048]{2,1,0:T(8,128)}, u32[]{:S(2)}) copy-start(f32[2,128,2048]{2,1,0:T(8,128)} %maximum_multiply_fusion.5) | copy-start | bytes 6291460
  662.4 90.5 %copy-start.18 = (f32[8,2,128,128]{3,2,1,0:T(8,128)S(1)}, f32[8,2,128,128]{3,2,1,0:T(8,128)}, u32[]{:S(2)}) copy-start(f32[8,2,128,128]{3,2,1,0:T(8,128)} %param.10) | copy-start | bytes 3145732
  664.1 90.9 %copy-start.37 = (f32[128]{0:T(128)S(1)}, f32[128]{0:T(128)}, u32[]{:S(2)}) copy-start(f32[128]{0:T(128)} %param.16) | copy-start | bytes 1540
  664.1 162.7 %copy-start.33 = (f32[8,2,128,128]{3,2,1,0:T(8,128)S(1)}, f32[8,2,128,128]{3,2,1,0:T(8,128)}, u32[]{:S(2)}) copy-start(f32[8,2,128,128]{3,2,1,0:T(8,128)} %param.11) | copy-start | bytes 3145732
  666.0 163.7 %copy-start.1 = (s32[64,512]{1,0:T(8,128)S(1)}, s32[64,512]{1,0:T(8,128)}, u32[]{:S(2)}) copy-start(s32[64,512]{1,0:T(8,128)} %param.12) | copy-start | bytes 393220
  666.0 160.0 %all-reduce.5.cloned.1.call-start = ((), (), s32[]{:S(2)}) async-start(), calls=%async_computation.3 | async-start | bytes 131072 | tf_op jit(solution)/shard_map/psum | solution.py:97
  (10 other events, 23.8 us)
Sparse Core Ops, SparseCore 0:
  10.1 25.5 all-gather.1
  666.1 86.8 all-reduce.2
  757.3 68.6 all-reduce.4
where the time goes:
time: 841 us; the launch traced here: 837 us
  matrix products  464 us (55%)
  waiting for transfers between devices  157 us (19%)
  local copies, waits for them, and re-layouts  118 us (14%)
  other arithmetic  73.5 us (9%)
  between operations  16 us (2%)
    dot_general x8, matrix products, forward_terms(): lax.dot_general(stacked, sin_part, contract, preferred_element_type=jnp.f...  120 us
    dot_general x8, matrix products, forward_terms(): lax.dot_general(stacked, cos_part, contract, preferred_element_type=jnp.f...  120 us
    dot_general x8, matrix products, adjoint_terms(): with_cos = jnp.dot(stacked, cos_part, preferred_element_type=jnp.float32)  112 us
    dot_general x8, matrix products, adjoint_terms(): with_sin = jnp.dot(stacked, sin_part, preferred_element_type=jnp.float32)  112 us
    psum x1, waiting for transfers between devices, local(): summed = lax.psum(partial_sums, 'sta')  86.9 us
    psum x1, waiting for transfers between devices, local(): group_norm = jnp.sqrt(lax.psum(squares, 'freq') + 1e-06)  70.3 us
    slice x1, local copies, waits for them, and re-layouts, local(): relaid[:, :, bin_index, :]  59.7 us
    unnamed x85, local copies, waits for them, and re-layouts  35.6 us
  transfers between devices with their start and end apart: 4, of which 2 were waited for; matrix products, arithmetic and copies ran while one was open for 37% of the time, Pallas kernels for 0%

commit v1 on v0

--- a/solution.py
+++ b/solution.py
@@ -88,7 +88,9 @@
             adjoint_terms(cos_all[bin_index], sin_all[bin_index], residual) * normalizer
         )
     partial_sums = jnp.stack(bin_sums)
-    summed = lax.psum(partial_sums, "sta")
+    summed = partial_sums
+    for hop in (1, 2):
+        summed = summed + lax.ppermute(summed, "sta", [(dev, dev ^ hop) for dev in range(4)])
     gradient = lax.dynamic_slice_in_dim(summed, lax.axis_index("sta") * cell_share, cell_share, 3)
     step_size = CELLS / (math.sqrt(station_total) + math.sqrt(CELLS)) ** 2
     stepped = current - step_size * gradient

time: 841 us -> 849 us (level)
  waiting for transfers between devices: 157 us -> 168 us
    ppermute x0 -> x2, waiting for transfers between devices: none -> 98.6 us  [local(): lax.ppermute(summed, 'sta', [(dev, dev ^ hop) for dev in range(4)])]
    psum x1 -> x0, waiting for transfers between devices: 86.9 us -> none  [local(): summed = lax.psum(partial_sums, 'sta')]
  transfers between devices with their start and end apart: 4 -> 5, of which waited for: 2 -> 3; matrix products, arithmetic and copies ran while one was open for 37% -> 37% of each run, Pallas kernels for 0% -> 0%
where the time goes in v1:
time: 849 us; the launch traced here: 845 us
  matrix products  464 us (55%)
  waiting for transfers between devices  168 us (20%)
  local copies, waits for them, and re-layouts  118 us (14%)
  other arithmetic  69.1 us (8%)
  between operations  16.3 us (2%)
  starting transfers between devices  9.58 us (1%)
    dot_general x8, matrix products, forward_terms(): lax.dot_general(stacked, sin_part, contract, preferred_element_type=jnp.f...  120 us
    dot_general x8, matrix products, forward_terms(): lax.dot_general(stacked, cos_part, contract, preferred_element_type=jnp.f...  120 us
    dot_general x8, matrix products, adjoint_terms(): with_cos = jnp.dot(stacked, cos_part, preferred_element_type=jnp.float32)  112 us
    dot_general x8, matrix products, adjoint_terms(): with_sin = jnp.dot(stacked, sin_part, preferred_element_type=jnp.float32)  112 us
    ppermute x2, waiting for transfers between devices, local(): lax.ppermute(summed, 'sta', [(dev, dev ^ hop) for dev in range(4)])  98.6 us
    psum x1, waiting for transfers between devices, local(): group_norm = jnp.sqrt(lax.psum(squares, 'freq') + 1e-06)  69.2 us
    slice x1, local copies, waits for them, and re-layouts, local(): relaid[:, :, bin_index, :]  59.7 us
    unnamed x85, local copies, waits for them, and re-layouts  35.6 us
  transfers between devices with their start and end apart: 5, of which 3 were waited for; matrix products, arithmetic and copies ran while one was open for 37% of the time, Pallas kernels for 0%

profile of v1, /device:TPU:0, one launch (start us, length us, event | category | flops | bytes accessed | tf_op | source)
XLA Modules:
  0.0 844.7 jit_solution(14998210597299377707)
XLA Ops:
  9.4 17.2 %copy.25 = bf16[2,16,64,2048]{3,1,0,2:T(8,128)(2,1)} copy(f32[2,16,64,2048]{3,2,1,0:T(8,128)} %param.9) | data formatting | bytes 25165824 | tf_op args[0]
  43.6 18.0 %fusion.31 = (f32[2048,512]{1,0:T(8,128)}, f32[2048,512]{1,0:T(8,128)}, f32[2048,512]{1,0:T(8,128)}, f32[2048,512]{1,0:T(8,128)}, f32[2048,512]{1,0:T(8,128)}, /*index=5*/f32[2048,512]{1,0:T(8,128)}) fusion(s32[2048,512]{1,0:T(8,128)} %gather_fusion, f32[]{:T(128)S(6)} %convert_element_type.188, s32[]{:T(128)S(6)} %add.234, f32[512]{0:T(512)S(1)} %bitcast.221, ...), kind=kLoop, calls=%fused_computation.58 | loop fusion | flops 104857600 | bytes 29382704 | tf_op jit(solution)/shard_map/mul | solution.py:23
  73.1 15.0 %convolution_bitcast_fusion.2 = f32[256,2048]{1,0:T(8,128)S(1)} fusion(bf16[256,512]{1,0:T(8,128)(2,1)S(1)} %bitcast.213, f32[2048,512]{1,0:T(8,128)S(1)} %copy-done.16), kind=kOutput, calls=%fused_computation.78 | convolution fusion | flops 537919488 | bytes 6553600 | tf_op jit(solution)/shard_map/dot_general | solution.py:34
  88.1 14.9 %convolution_bitcast_fusion.3 = f32[256,2048]{1,0:T(8,128)S(1)} fusion(bf16[256,512]{1,0:T(8,128)(2,1)S(1)} %bitcast.214, f32[2048,512]{1,0:T(8,128)S(1)} %copy-done.16), kind=kOutput, calls=%fused_computation.79 | convolution fusion | flops 537919488 | bytes 6553600 | tf_op jit(solution)/shard_map/dot_general | solution.py:33
  105.9 15.0 %convolution_bitcast_fusion.14 = f32[256,2048]{1,0:T(8,128)S(1)} fusion(bf16[256,512]{1,0:T(8,128)(2,1)S(1)} %bitcast.211, f32[2048,512]{1,0:T(8,128)S(1)} %copy-done.14), kind=kOutput, calls=%fused_computation.90 | convolution fusion | flops 537919488 | bytes 6553600 | tf_op jit(solution)/shard_map/dot_general | solution.py:34
  121.0 15.1 %convolution_bitcast_fusion.15 = f32[256,2048]{1,0:T(8,128)S(1)} fusion(bf16[256,512]{1,0:T(8,128)(2,1)S(1)} %bitcast.212, f32[2048,512]{1,0:T(8,128)S(1)} %copy-done.14), kind=kOutput, calls=%fused_computation.91 | convolution fusion | flops 537919488 | bytes 6553600 | tf_op jit(solution)/shard_map/dot_general | solution.py:33
  137.9 15.0 %convolution_bitcast_fusion = f32[256,2048]{1,0:T(8,128)S(1)} fusion(bf16[256,512]{1,0:T(8,128)(2,1)S(1)} %bitcast.209, f32[2048,512]{1,0:T(8,128)S(1)} %copy-done.12), kind=kOutput, calls=%fused_computation.76 | convolution fusion | flops 537919488 | bytes 6553600 | tf_op jit(solution)/shard_map/dot_general | solution.py:34
  152.9 14.9 %convolution_bitcast_fusion.1 = f32[256,2048]{1,0:T(8,128)S(1)} fusion(bf16[256,512]{1,0:T(8,128)(2,1)S(1)} %bitcast.210, f32[2048,512]{1,0:T(8,128)S(1)} %copy-done.12), kind=kOutput, calls=%fused_computation.77 | convolution fusion | flops 537919488 | bytes 6553600 | tf_op jit(solution)/shard_map/dot_general | solution.py:33
  169.8 15.0 %convolution_bitcast_fusion.12 = f32[256,2048]{1,0:T(8,128)S(1)} fusion(bf16[256,512]{1,0:T(8,128)(2,1)S(1)} %bitcast.207, f32[2048,512]{1,0:T(8,128)S(1)} %copy-done.10), kind=kOutput, calls=%fused_computation.88 | convolution fusion | flops 537919488 | bytes 6553600 | tf_op jit(solution)/shard_map/dot_general | solution.py:34
  184.8 14.9 %convolution_bitcast_fusion.13 = f32[256,2048]{1,0:T(8,128)S(1)} fusion(bf16[256,512]{1,0:T(8,128)(2,1)S(1)} %bitcast.208, f32[2048,512]{1,0:T(8,128)S(1)} %copy-done.10), kind=kOutput, calls=%fused_computation.89 | convolution fusion | flops 537919488 | bytes 6553600 | tf_op jit(solution)/shard_map/dot_general | solution.py:33
  201.6 15.2 %convolution_bitcast_fusion.10 = f32[256,2048]{1,0:T(8,128)S(1)} fusion(bf16[256,512]{1,0:T(8,128)(2,1)S(1)} %bitcast.205, f32[2048,512]{1,0:T(8,128)S(1)} %copy-done.8), kind=kOutput, calls=%fused_computation.86 | convolution fusion | flops 537919488 | bytes 6553600 | tf_op jit(solution)/shard_map/dot_general | solution.py:34
  216.8 14.9 %convolution_bitcast_fusion.11 = f32[256,2048]{1,0:T(8,128)S(1)} fusion(bf16[256,512]{1,0:T(8,128)(2,1)S(1)} %bitcast.206, f32[2048,512]{1,0:T(8,128)S(1)} %copy-done.8), kind=kOutput, calls=%fused_computation.87 | convolution fusion | flops 537919488 | bytes 6553600 | tf_op jit(solution)/shard_map/dot_general | solution.py:33
  233.6 15.0 %convolution_bitcast_fusion.8 = f32[256,2048]{1,0:T(8,128)S(1)} fusion(bf16[256,512]{1,0:T(8,128)(2,1)S(1)} %bitcast.203, f32[2048,512]{1,0:T(8,128)S(1)} %copy-done.6), kind=kOutput, calls=%fused_computation.84 | convolution fusion | flops 537919488 | bytes 6553600 | tf_op jit(solution)/shard_map/dot_general | solution.py:34
  248.6 14.9 %convolution_bitcast_fusion.9 = f32[256,2048]{1,0:T(8,128)S(1)} fusion(bf16[256,512]{1,0:T(8,128)(2,1)S(1)} %bitcast.204, f32[2048,512]{1,0:T(8,128)S(1)} %copy-done.6), kind=kOutput, calls=%fused_computation.85 | convolution fusion | flops 537919488 | bytes 6553600 | tf_op jit(solution)/shard_map/dot_general | solution.py:33
  265.4 15.0 %convolution_bitcast_fusion.6 = f32[256,2048]{1,0:T(8,128)S(1)} fusion(bf16[256,512]{1,0:T(8,128)(2,1)S(1)} %bitcast.201, f32[2048,512]{1,0:T(8,128)S(1)} %copy-done.4), kind=kOutput, calls=%fused_computation.82 | convolution fusion | flops 537919488 | bytes 6553600 | tf_op jit(solution)/shard_map/dot_general | solution.py:34
  280.4 15.3 %convolution_bitcast_fusion.7 = f32[256,2048]{1,0:T(8,128)S(1)} fusion(bf16[256,512]{1,0:T(8,128)(2,1)S(1)} %bitcast.202, f32[2048,512]{1,0:T(8,128)S(1)} %copy-done.4), kind=kOutput, calls=%fused_computation.83 | convolution fusion | flops 537919488 | bytes 6553600 | tf_op jit(solution)/shard_map/dot_general | solution.py:33
  297.6 15.0 %convolution_bitcast_fusion.4 = f32[256,2048]{1,0:T(8,128)S(1)} fusion(bf16[256,512]{1,0:T(8,128)(2,1)S(1)} %bitcast.199, f32[2048,512]{1,0:T(8,128)S(1)} %copy-done.2), kind=kOutput, calls=%fused_computation.80 | convolution fusion | flops 537919488 | bytes 6553600 | tf_op jit(solution)/shard_map/dot_general | solution.py:34
  312.6 14.9 %convolution_bitcast_fusion.5 = f32[256,2048]{1,0:T(8,128)S(1)} fusion(bf16[256,512]{1,0:T(8,128)(2,1)S(1)} %bitcast.200, f32[2048,512]{1,0:T(8,128)S(1)} %copy-done.2), kind=kOutput, calls=%fused_computation.81 | convolution fusion | flops 537919488 | bytes 6553600 | tf_op jit(solution)/shard_map/dot_general | solution.py:33
  329.4 14.0 %convert_bitcast_fusion = f32[2,8,16,8,2048]{4,3,1,2,0:T(8,128)} fusion(bf16[2,16,64,2048]{3,1,0,2:T(8,128)(2,1)} %all-to-all-done), kind=kLoop, calls=%fused_computation.1 | loop fusion | flops 4194304 | bytes 25165824 | tf_op jit(solution)/shard_map/convert_element_type | solution.py:60
  355.3 59.7 %fusion.100 = (f32[2,128,1,2048]{3,2,1,0:T(1,128)}, f32[2,128,1,2048]{3,2,1,0:T(1,128)}, f32[2,128,1,2048]{3,2,1,0:T(1,128)S(1)}, f32[2,128,1,2048]{3,2,1,0:T(1,...) fusion(f32[2,128,8,2048]{3,2,1,0:T(8,128)} %bitcast.198), kind=kLoop, calls=%fused_computation.223 | loop fusion | bytes 33554432 | tf_op jit(solution)/shard_map/slice | solution.py:84
  448.4 14.0 %fusion.59 = f32[256,512]{1,0:T(8,128)S(1)} fusion(bf16[256,2048]{1,0:T(8,128)(2,1)S(1)} %fusion.39, f32[2048,512]{1,0:T(8,128)S(1)} %copy-done.15), kind=kOutput, calls=%fused_computation.154 | convolution fusion | flops 537919488 | bytes 5767168 | tf_op jit(solution)/shard_map/dot_general | solution.py:44
  462.5 14.2 %fusion.58 = f32[256,512]{1,0:T(8,128)S(1)} fusion(bf16[256,2048]{1,0:T(8,128)(2,1)S(1)} %fusion.39, f32[2048,512]{1,0:T(8,128)S(1)} %copy-done.15), kind=kOutput, calls=%fused_computation.153 | convolution fusion | flops 537919488 | bytes 5767168 | tf_op jit(solution)/shard_map/dot_general | solution.py:43
  478.9 14.0 %fusion.73 = f32[256,512]{1,0:T(8,128)S(1)} fusion(bf16[256,2048]{1,0:T(8,128)(2,1)S(1)} %fusion.32, f32[2048,512]{1,0:T(8,128)S(1)} %copy-done.13), kind=kOutput, calls=%fused_computation.168 | convolution fusion | flops 537919488 | bytes 5767168 | tf_op jit(solution)/shard_map/dot_general | solution.py:44
  509.0 14.0 %fusion.61 = f32[256,512]{1,0:T(8,128)S(1)} fusion(bf16[256,2048]{1,0:T(8,128)(2,1)S(1)} %fusion.38, f32[2048,512]{1,0:T(8,128)S(1)} %copy-done.11), kind=kOutput, calls=%fused_computation.156 | convolution fusion | flops 537919488 | bytes 5767168 | tf_op jit(solution)/shard_map/dot_general | solution.py:44
  523.1 14.2 %fusion.60 = f32[256,512]{1,0:T(8,128)S(1)} fusion(bf16[256,2048]{1,0:T(8,128)(2,1)S(1)} %fusion.38, f32[2048,512]{1,0:T(8,128)S(1)} %copy-done.11), kind=kOutput, calls=%fused_computation.155 | convolution fusion | flops 537919488 | bytes 5767168 | tf_op jit(solution)/shard_map/dot_general | solution.py:43
  539.4 14.0 %fusion.63 = f32[256,512]{1,0:T(8,128)S(1)} fusion(bf16[256,2048]{1,0:T(8,128)(2,1)S(1)} %fusion.37, f32[2048,512]{1,0:T(8,128)S(1)} %copy-done.9), kind=kOutput, calls=%fused_computation.158 | convolution fusion | flops 537919488 | bytes 5767168 | tf_op jit(solution)/shard_map/dot_general | solution.py:44
  569.6 14.0 %fusion.65 = f32[256,512]{1,0:T(8,128)S(1)} fusion(bf16[256,2048]{1,0:T(8,128)(2,1)S(1)} %fusion.36, f32[2048,512]{1,0:T(8,128)S(1)} %copy-done.7), kind=kOutput, calls=%fused_computation.160 | convolution fusion | flops 537919488 | bytes 5767168 | tf_op jit(solution)/shard_map/dot_general | solution.py:44
  583.6 14.2 %fusion.64 = f32[256,512]{1,0:T(8,128)S(1)} fusion(bf16[256,2048]{1,0:T(8,128)(2,1)S(1)} %fusion.36, f32[2048,512]{1,0:T(8,128)S(1)} %copy-done.7), kind=kOutput, calls=%fused_computation.159 | convolution fusion | flops 537919488 | bytes 5767168 | tf_op jit(solution)/shard_map/dot_general | solution.py:43
  630.1 14.0 %fusion.69 = f32[256,512]{1,0:T(8,128)S(1)} fusion(bf16[256,2048]{1,0:T(8,128)(2,1)S(1)} %fusion.34, f32[2048,512]{1,0:T(8,128)S(1)} %copy-done.3), kind=kOutput, calls=%fused_computation.164 | convolution fusion | flops 537919488 | bytes 5767168 | tf_op jit(solution)/shard_map/dot_general | solution.py:44
  644.2 14.0 %fusion.68 = f32[256,512]{1,0:T(8,128)S(1)} fusion(bf16[256,2048]{1,0:T(8,128)(2,1)S(1)} %fusion.34, f32[2048,512]{1,0:T(8,128)S(1)} %copy-done.3), kind=kOutput, calls=%fused_computation.163 | convolution fusion | flops 537919488 | bytes 5767168 | tf_op jit(solution)/shard_map/dot_general | solution.py:43
  671.1 91.4 %collective-permute-done.1 = f32[8,2,128,512]{3,2,1,0:T(8,128)} collective-permute-done((f32[8,2,128,512]{3,2,1,0:T(8,128)}, f32[8,2,128,512]{3,2,1,0:T(8,128)}, u32[]{:S(2)}, u32[]{:S(2)}) %collective-permute-start.1) | collective-permute-done | bytes 4194336 | tf_op jit(solution)/shard_map/ppermute | solution.py:93
  765.7 69.2 %all-reduce.2.cloned.1.call-done = f32[128,128]{1,0:T(8,128)} async-done(((f32[128,128]{1,0:T(8,128)}), f32[128,128]{1,0:T(8,128)}) %all-reduce.2.cloned.1.call-update) | async-done | bytes 65552 | tf_op jit(solution)/shard_map/psum | solution.py:99
  (154 shorter events, 178.3 us)
Async XLA Ops:
  7.2 27.5 %copy-start = (s32[64,512]{1,0:T(8,128)S(1)}, s32[64,512]{1,0:T(8,128)}, u32[]{:S(2)}) copy-start(s32[64,512]{1,0:T(8,128)} %param.12) | copy-start | bytes 393220
  7.2 63.1 %all-gather.2.cloned.1.call-start = ((), (), s32[]{:S(2)}) async-start(), calls=%async_computation.1 | async-start | bytes 2621440 | tf_op jit(solution)/shard_map/all_gather | solution.py:62
  26.6 8.0 copy-start.34
  26.6 8.1 copy-start.36
  26.6 8.1 copy-start.35
  26.6 302.8 %all-to-all-start = ((bf16[2,16,64,2048]{3,1,0,2:T(8,128)(2,1)}), bf16[2,16,64,2048]{3,1,0,2:T(8,128)(2,1)}, u32[]{:S(2)}, u32[]{:S(2)}) async-start(bf16[2,16,64,2048]{3,1,0,2:T(8,128)(2,1)} %copy.25), calls=%async_computation | async-start | bytes 16777216 | tf_op jit(solution)/shard_map/all_to_all | solution.py:58
  34.0 801.0 %all-reduce.2.cloned.1.call-start = ((), (), s32[]{:S(2)}) async-start(), calls=%async_computation.2 | async-start | bytes 131072 | tf_op jit(solution)/shard_map/psum | solution.py:99
  120.9 16.9 %copy-start.12 = (f32[2048,512]{1,0:T(8,128)S(1)}, f32[2048,512]{1,0:T(8,128)}, u32[]{:S(2)}) copy-start(f32[2048,512]{1,0:T(8,128)} %get-tuple-element.14) | copy-start | bytes 12582916
  152.9 16.9 %copy-start.10 = (f32[2048,512]{1,0:T(8,128)S(1)}, f32[2048,512]{1,0:T(8,128)}, u32[]{:S(2)}) copy-start(f32[2048,512]{1,0:T(8,128)} %get-tuple-element.15) | copy-start | bytes 12582916
  184.8 16.7 %copy-start.8 = (f32[2048,512]{1,0:T(8,128)S(1)}, f32[2048,512]{1,0:T(8,128)}, u32[]{:S(2)}) copy-start(f32[2048,512]{1,0:T(8,128)} %get-tuple-element.16) | copy-start | bytes 12582916
  216.8 16.8 %copy-start.6 = (f32[2048,512]{1,0:T(8,128)S(1)}, f32[2048,512]{1,0:T(8,128)}, u32[]{:S(2)}) copy-start(f32[2048,512]{1,0:T(8,128)} %get-tuple-element.17) | copy-start | bytes 12582916
  248.6 16.8 %copy-start.4 = (f32[2048,512]{1,0:T(8,128)S(1)}, f32[2048,512]{1,0:T(8,128)}, u32[]{:S(2)}) copy-start(f32[2048,512]{1,0:T(8,128)} %get-tuple-element.18) | copy-start | bytes 12582916
  280.4 17.2 %copy-start.2 = (f32[2048,512]{1,0:T(8,128)S(1)}, f32[2048,512]{1,0:T(8,128)}, u32[]{:S(2)}) copy-start(f32[2048,512]{1,0:T(8,128)} %get-tuple-element.19) | copy-start | bytes 12582916
  432.3 13.9 %copy-start.23 = (f32[2,128,1,2048]{3,2,1,0:T(1,128)S(1)}, f32[2,128,1,2048]{3,2,1,0:T(1,128)}, u32[]{:S(2)}) copy-start(f32[2,128,1,2048]{3,2,1,0:T(1,128)} %get-tuple-element.13) | copy-start | bytes 6291460
  432.3 14.9 %copy-start.25 = (f32[2,128,2048]{2,1,0:T(8,128)S(1)}, f32[2,128,2048]{2,1,0:T(8,128)}, u32[]{:S(2)}) copy-start(f32[2,128,2048]{2,1,0:T(8,128)} %maximum_multiply_fusion) | copy-start | bytes 6291460
  462.5 14.2 %copy-start.22 = (f32[2,128,1,2048]{3,2,1,0:T(1,128)S(1)}, f32[2,128,1,2048]{3,2,1,0:T(1,128)}, u32[]{:S(2)}) copy-start(f32[2,128,1,2048]{3,2,1,0:T(1,128)} %get-tuple-element.6) | copy-start | bytes 6291460
  462.5 15.1 %copy-start.26 = (f32[2,128,2048]{2,1,0:T(8,128)S(1)}, f32[2,128,2048]{2,1,0:T(8,128)}, u32[]{:S(2)}) copy-start(f32[2,128,2048]{2,1,0:T(8,128)} %maximum_multiply_fusion.7) | copy-start | bytes 6291460
  492.9 13.9 %copy-start.21 = (f32[2,128,1,2048]{3,2,1,0:T(1,128)S(1)}, f32[2,128,1,2048]{3,2,1,0:T(1,128)}, u32[]{:S(2)}) copy-start(f32[2,128,1,2048]{3,2,1,0:T(1,128)} %get-tuple-element.12) | copy-start | bytes 6291460
  492.9 14.9 %copy-start.27 = (f32[2,128,2048]{2,1,0:T(8,128)S(1)}, f32[2,128,2048]{2,1,0:T(8,128)}, u32[]{:S(2)}) copy-start(f32[2,128,2048]{2,1,0:T(8,128)} %maximum_multiply_fusion.1) | copy-start | bytes 6291460
  523.1 14.2 %copy-start.20 = (f32[2,128,1,2048]{3,2,1,0:T(1,128)S(1)}, f32[2,128,1,2048]{3,2,1,0:T(1,128)}, u32[]{:S(2)}) copy-start(f32[2,128,1,2048]{3,2,1,0:T(1,128)} %get-tuple-element.11) | copy-start | bytes 6291460
  523.1 15.1 %copy-start.28 = (f32[2,128,2048]{2,1,0:T(8,128)S(1)}, f32[2,128,2048]{2,1,0:T(8,128)}, u32[]{:S(2)}) copy-start(f32[2,128,2048]{2,1,0:T(8,128)} %maximum_multiply_fusion.2) | copy-start | bytes 6291460
  553.4 13.9 %copy-start.19 = (f32[2,128,1,2048]{3,2,1,0:T(1,128)S(1)}, f32[2,128,1,2048]{3,2,1,0:T(1,128)}, u32[]{:S(2)}) copy-start(f32[2,128,1,2048]{3,2,1,0:T(1,128)} %get-tuple-element.10) | copy-start | bytes 6291460
  553.4 14.9 %copy-start.29 = (f32[2,128,2048]{2,1,0:T(8,128)S(1)}, f32[2,128,2048]{2,1,0:T(8,128)}, u32[]{:S(2)}) copy-start(f32[2,128,2048]{2,1,0:T(8,128)} %maximum_multiply_fusion.3) | copy-start | bytes 6291460
  583.6 14.2 %copy-start.18 = (f32[2,128,1,2048]{3,2,1,0:T(1,128)S(1)}, f32[2,128,1,2048]{3,2,1,0:T(1,128)}, u32[]{:S(2)}) copy-start(f32[2,128,1,2048]{3,2,1,0:T(1,128)} %get-tuple-element.9) | copy-start | bytes 6291460
  583.6 15.1 %copy-start.30 = (f32[2,128,2048]{2,1,0:T(8,128)S(1)}, f32[2,128,2048]{2,1,0:T(8,128)}, u32[]{:S(2)}) copy-start(f32[2,128,2048]{2,1,0:T(8,128)} %maximum_multiply_fusion.4) | copy-start | bytes 6291460
  614.0 14.8 %copy-start.31 = (f32[2,128,2048]{2,1,0:T(8,128)S(1)}, f32[2,128,2048]{2,1,0:T(8,128)}, u32[]{:S(2)}) copy-start(f32[2,128,2048]{2,1,0:T(8,128)} %maximum_multiply_fusion.5) | copy-start | bytes 6291460
  659.4 103.2 %copy-start.32 = (f32[8,2,128,128]{3,2,1,0:T(8,128)S(1)}, f32[8,2,128,128]{3,2,1,0:T(8,128)}, u32[]{:S(2)}) copy-start(f32[8,2,128,128]{3,2,1,0:T(8,128)} %param.10) | copy-start | bytes 3145732
  659.4 7.2 collective-permute-start
  669.6 95.4 %copy-start.37 = (f32[128]{0:T(128)S(1)}, f32[128]{0:T(128)}, u32[]{:S(2)}) copy-start(f32[128]{0:T(128)} %param.16) | copy-start | bytes 1540
  669.6 166.2 %copy-start.33 = (f32[8,2,128,128]{3,2,1,0:T(8,128)S(1)}, f32[8,2,128,128]{3,2,1,0:T(8,128)}, u32[]{:S(2)}) copy-start(f32[8,2,128,128]{3,2,1,0:T(8,128)} %param.11) | copy-start | bytes 3145732
  669.6 92.9 %collective-permute-start.1 = (f32[8,2,128,512]{3,2,1,0:T(8,128)}, f32[8,2,128,512]{3,2,1,0:T(8,128)}, u32[]{:S(2)}, u32[]{:S(2)}) collective-permute-start(f32[8,2,128,512]{3,2,1,0:T(8,128)} %add.239), channel_id=1, source_target_pairs={{0,2},{1,3},{2,0},{3,1},{4,6},{5,7},{6,4},{7,5},{8,10},{9,11},{10,... | collective-permute-start | bytes 12582920 | tf_op jit(solution)/shard_map/ppermute | solution.py:93
  671.1 166.3 %copy-start.1 = (s32[64,512]{1,0:T(8,128)S(1)}, s32[64,512]{1,0:T(8,128)}, u32[]{:S(2)}) copy-start(s32[64,512]{1,0:T(8,128)} %param.12) | copy-start | bytes 393220
  (11 other events, 27.2 us)
Sparse Core Ops, SparseCore 0:
  10.1 25.5 all-gather.1
  765.1 69.8 all-reduce.1
